TPU v7x, 256 devices: a whole 4x4x8 slice. The times are simulated.
256 devices in a mesh: dp: 4 (over z_lo), ctx: 64 (over z_hi, y, x, core).
Axes of the slice: x: 4, y: 4, z: 8 (z_hi: 2, z_lo: 4; z = z_hi * 4 + z_lo), core: 2. Of those that a mesh axis runs over, the one named last changes fastest.
Arguments:
- qkv: bfloat16 [4, 8192, 6144], P('dp', 'ctx'), may hold values from -6 to 6
- short_filter: float32 [7, 768], replicated, may hold values from -2 to 2
- long_filter: float32 [2048, 8192], P('ctx'), may hold values from -1.1 to 1.1
- cotangent: bfloat16 [4, 8192, 2048], P('dp', 'ctx'), may hold values from -6 to 6
Outputs:
- mixer_out: bfloat16 [4, 8192, 2048], P('dp', 'ctx')
- grad_qkv: bfloat16 [4, 8192, 6144], P('dp', 'ctx')
- grad_long: float32 [2048, 8192], P('ctx')
- grad_short: float32 [7, 768], replicated
All inputs are finite; a program needn't handle non-finite values.
Results may differ from a plain program's by a relative error of at most 0.014.
Values may be sent and summed in bfloat16 or wider, within the bound.
No kernel may reach another device: no remote copies, remote signals or barrier semaphores. Data moves between devices by JAX's collectives and lax.ppermute only.
A program may use at most 128 MiB of HBM per device.

v0:
```python
import math
import jax
import jax.numpy as jnp
from jax import lax
from jax.sharding import PartitionSpec as P

precise = lax.Precision.HIGHEST


def from_behind(array, axis, by):
    devices = lax.axis_size(axis)
    pairs = [(i, i + by) for i in range(devices) if 0 <= i + by < devices]
    return lax.ppermute(array, axis, pairs)


def angles(row_count, col_count, period):
    row_iota = lax.broadcasted_iota(jnp.int32, (row_count, col_count), 0)
    col_iota = lax.broadcasted_iota(jnp.int32, (row_count, col_count), 1)
    return (row_iota * col_iota % period).astype(jnp.float32) * (2.0 * math.pi / period)


def matmul(left_side, right_side):
    return jnp.dot(left_side, right_side, precision=precise, preferred_element_type=jnp.float32)


def column_table(col_count, sign_flip):
    angle_cols = angles(col_count, col_count, col_count)
    cos_part = jnp.cos(angle_cols)
    sin_part = sign_flip * jnp.sin(angle_cols)
    upper = jnp.concatenate([cos_part, sin_part], axis=1)
    lower = jnp.concatenate([-sin_part, cos_part], axis=1)
    return jnp.concatenate([upper, lower], axis=0)


def forward_transform(signal):
    half_rows, own_chans, col_count = signal.shape
    row_count = 2 * half_rows
    total_len = row_count * col_count
    angle_rows = angles(row_count, half_rows, row_count)
    row_table = jnp.concatenate([jnp.cos(angle_rows), -jnp.sin(angle_rows)], axis=0)
    rows_out = matmul(
        row_table, signal.reshape(half_rows, own_chans * col_count).astype(jnp.float32)
    )
    rows_out = rows_out.reshape(2, row_count, own_chans, col_count)
    part_real = rows_out[0]
    part_imag = rows_out[1]
    twist = angles(row_count, col_count, total_len)[:, None, :]
    twist_real = jnp.cos(twist)
    twist_imag = -jnp.sin(twist)
    turned = jnp.concatenate(
        [
            part_real * twist_real - part_imag * twist_imag,
            part_real * twist_imag + part_imag * twist_real,
        ],
        axis=2,
    )
    spec = matmul(
        turned.reshape(row_count * own_chans, 2 * col_count), column_table(col_count, -1.0)
    )
    return spec.reshape(row_count, own_chans, 2 * col_count)


def inverse_transform(spec):
    row_count, own_chans, double_cols = spec.shape
    col_count = double_cols // 2
    half_rows = row_count // 2
    total_len = row_count * col_count
    back = matmul(spec.reshape(row_count * own_chans, double_cols), column_table(col_count, 1.0))
    back = back.reshape(row_count, own_chans, double_cols)
    back_real = back[:, :, :col_count]
    back_imag = back[:, :, col_count:]
    twist = angles(row_count, col_count, total_len)[:, None, :]
    twist_real = jnp.cos(twist)
    twist_imag = jnp.sin(twist)
    turned = jnp.concatenate(
        [
            back_real * twist_real - back_imag * twist_imag,
            back_real * twist_imag + back_imag * twist_real,
        ],
        axis=0,
    )
    angle_rows = angles(half_rows, row_count, row_count)
    row_table = jnp.concatenate([jnp.cos(angle_rows), -jnp.sin(angle_rows)], axis=1) * (
        1.0 / total_len
    )
    result = matmul(row_table, turned.reshape(2 * row_count, own_chans * col_count))
    return result.reshape(half_rows, own_chans, col_count)


def spec_times(first_spec, second_spec, conjugate):
    col_count = first_spec.shape[2] // 2
    first_real = first_spec[:, :, :col_count]
    first_imag = first_spec[:, :, col_count:]
    second_real = second_spec[:, :, :col_count]
    second_imag = conjugate * second_spec[:, :, col_count:]
    return jnp.concatenate(
        [
            first_real * second_real - first_imag * second_imag,
            first_real * second_imag + first_imag * second_real,
        ],
        axis=2,
    )


def shards(qkv, short_filter, long_filter, cotangent):
    seq_rows = qkv[0]
    row_count, width_all = seq_rows.shape
    width = width_all // 3
    tap_count = short_filter.shape[0]
    group_size = width_all // short_filter.shape[1]
    ctx_count = lax.axis_size("ctx")
    own_chans = width // ctx_count
    grad_scale = 1.0 / math.sqrt(lax.axis_size("dp") * ctx_count * row_count)
    tap_weights = jnp.repeat(short_filter, group_size, axis=1)
    left_rim = from_behind(seq_rows[row_count - tap_count + 1 :], "ctx", 1)
    padded = jnp.concatenate([left_rim, seq_rows], axis=0).astype(jnp.float32)
    short_out = jnp.zeros((row_count, width_all), jnp.float32)
    for lag_index in range(tap_count):
        start = tap_count - 1 - lag_index
        short_out = short_out + tap_weights[lag_index] * padded[start : start + row_count]
    query_rows = short_out[:, :width]
    key_rows = short_out[:, width : 2 * width]
    value_rows = short_out[:, 2 * width :]
    cot_rows = cotangent[0].astype(jnp.float32)
    product = (key_rows * value_rows).T.astype(jnp.bfloat16)[None]
    grad_out = (cot_rows * query_rows).T.astype(jnp.bfloat16)[None]
    filter_taps = long_filter.reshape(own_chans, ctx_count, row_count).transpose(1, 0, 2)
    filter_spec = forward_transform(filter_taps)
    own_prod = lax.all_to_all(product, "ctx", split_axis=1, concat_axis=0, tiled=True)
    prod_spec = forward_transform(own_prod)
    y_own = inverse_transform(spec_times(prod_spec, filter_spec, 1.0))
    y_own, prod_spec = (y_own.astype(jnp.bfloat16), prod_spec)
    long_back = lax.all_to_all(y_own, "ctx", split_axis=0, concat_axis=1, tiled=True)
    own_grad = lax.all_to_all(grad_out, "ctx", split_axis=1, concat_axis=0, tiled=True)
    grad_spec = forward_transform(own_grad)
    du_own = inverse_transform(spec_times(grad_spec, filter_spec, -1.0))
    dh_own = inverse_transform(spec_times(grad_spec, prod_spec, -1.0))
    du_own, dh_own = (du_own.astype(jnp.bfloat16), dh_own)
    du_back = lax.all_to_all(du_own, "ctx", split_axis=0, concat_axis=1, tiled=True)
    long_rows = long_back[0].T.astype(jnp.float32)
    mixer_out = (query_rows * long_rows).astype(jnp.bfloat16)[None]
    grad_prod = du_back[0].T.astype(jnp.float32)
    grad_short_out = jnp.concatenate(
        [cot_rows * long_rows, grad_prod * value_rows, grad_prod * key_rows], axis=1
    )
    right_rim = from_behind(grad_short_out[: tap_count - 1].astype(jnp.bfloat16), "ctx", -1).astype(
        jnp.float32
    )
    grad_padded = jnp.concatenate([grad_short_out, right_rim], axis=0)
    grad_rows = jnp.zeros((row_count, width_all), jnp.float32)
    for lag_index in range(tap_count):
        grad_rows = (
            grad_rows + tap_weights[lag_index] * grad_padded[lag_index : lag_index + row_count]
        )
    grad_qkv = grad_rows.astype(jnp.bfloat16)[None]
    lag_terms = []
    for lag_index in range(tap_count):
        start = tap_count - 1 - lag_index
        lag_terms.append(jnp.sum(grad_short_out * padded[start : start + row_count], axis=0))
    short_terms = jnp.stack(lag_terms).reshape(tap_count, -1, group_size).sum(axis=2) * grad_scale
    long_terms = dh_own.transpose(1, 0, 2).reshape(own_chans, ctx_count * row_count) * grad_scale
    grad_short = lax.psum(short_terms, ("dp", "ctx"))
    grad_long = lax.psum(long_terms.astype(jnp.bfloat16), "dp").astype(jnp.float32)
    return (mixer_out, grad_qkv, grad_long, grad_short)


def solution(mesh):
    return jax.shard_map(
        shards,
        mesh=mesh,
        in_specs=(P("dp", "ctx", None), P(), P("ctx", None), P("dp", "ctx", None)),
        out_specs=(P("dp", "ctx", None), P("dp", "ctx", None), P("ctx", None), P()),
        check_vma=False,
    )
```

profile of v0, /device:TPU:1, one launch (start us, length us, event | category | flops | bytes accessed | tf_op | source)
XLA Modules:
  0.0 534.2 jit_solution(974061488572454364)
XLA Ops:
  15.1 5.7 %fusion.53 = f32[256,4096]{1,0:T(8,128)} fusion(f32[8,8,32,128]{3,2,1,0:T(8,128)S(1)} %bitcast.145, f32[128,64]{1,0:T(8,128)S(1)} %get-tuple-element.64, f32[128,64]{1,0:T(8,128)S(1)} %get-tuple-element.65), kind=kOutput, calls=%fused_computation.90 | convolution fusion | flops 805322752 | bytes 5308416 | tf_op jit(solution)/shard_map/dot_general | solution.py:23
  28.0 11.8 %multiply_add_fusion = f32[128,6144]{0,1:T(8,128)S(1)} fusion(f32[134,6144]{0,1:T(8,128)S(1)} %maximum_convert_fusion, f32[6144]{0:T(1024)S(1)} %broadcast_in_dim.60, f32[6144]{0:T(1024)S(1)} %broadcast_in_dim.58, f32[6144]{0:T(1024)S(1)} %broadcast_in_dim.56, f32[6144]{0:T(1024)S(1)} %broadcast_in_dim.54, f32[6144]{0:T(1024)S(1)} %broadcast_in_dim.52, ...), kind=kLoop, calls=%fused_computation.57 | loop fusion | flops 10223616 | bytes 25337856 | tf_op jit(solution)/shard_map/add | solution.py:120
  41.6 8.1 %copy.95 = bf16[1,2048,128]{2,0,1:T(2,128)(2,1)S(1)} copy(bf16[1,2048,128]{2,1,0:T(8,128)(2,1)S(1)} %fusion.62) | data formatting | bytes 1048576 | tf_op jit(solution)/shard_map/broadcast_in_dim | solution.py:126
  50.2 12.0 %reduce.18 = bf16[2048,128]{1,0:T(8,128)(2,1)S(1)} reduce(bf16[2048,1,128]{2,1,0:T(2,128)(2,1)S(1)} %bitcast.143, bf16[]{:T(256)} %broadcast.244), dimensions={1}, to_apply=%bitcast.134.reduce_sub_computation | reduce | bytes 1048578
  63.1 14.1 %all-to-all-start.2 = ((bf16[64,2,2048]{2,1,0:T(2,128)(2,1)}), bf16[64,2,2048]{2,1,0:T(2,128)(2,1)}, u32[]{:S(2)}, u32[]{:S(2)}) async-start(bf16[64,2,2048]{2,1,0:T(2,128)(2,1)} %reshape.246), calls=%async_computation.2 | async-start | bytes 1048576 | tf_op jit(solution)/shard_map/all_to_all | solution.py:134
  98.1 8.8 %bitcast_reduce_fusion.1 = bf16[2048,128]{1,0:T(8,128)(2,1)S(1)} fusion(bf16[2048,1,128]{2,1,0:T(2,128)(2,1)S(1)} %reshape.247), kind=kLoop, calls=%fused_computation.202 | loop fusion | bytes 1048576 | tf_op jit(solution)/shard_map/all_to_all | solution.py:134
  139.9 5.6 %copy.63 = f32[256,32,128]{0,2,1:T(8,128)} copy(f32[256,32,128]{2,0,1:T(8,128)} %pad_maximum_fusion.2) | data formatting | bytes 8388608 | tf_op jit(solution)/shard_map/concatenate | solution.py:75
  145.5 6.4 %fusion.49 = bf16[64,32,128]{2,0,1:T(8,128)(2,1)S(1)} fusion(f32[256,32,128]{0,2,1:T(8,128)} %copy.63, f32[64,128]{1,0:T(8,128)S(1)} %copy-done.20, f32[64,128]{1,0:T(8,128)S(1)} %copy-done.22), kind=kOutput, calls=%fused_computation.88 | convolution fusion | flops 805601280 | bytes 4784128 | tf_op jit(solution)/shard_map/dot_general | solution.py:23
  152.3 29.5 %all_to_all.16 = bf16[64,32,128]{2,1,0:T(8,128)(2,1)S(1)} all-to-all(bf16[64,32,128]{2,1,0:T(8,128)(2,1)S(1)} %copy.64), channel_id=1, replica_groups=mesh['dp'=4,'ctx'=64] {'ctx'}, dimensions={0} | all-to-all | bytes 1048576 | tf_op jit(solution)/shard_map/all_to_all | solution.py:139
  182.0 8.1 %copy.96 = bf16[1,2048,128]{2,0,1:T(2,128)(2,1)S(1)} copy(bf16[1,2048,128]{2,1,0:T(8,128)(2,1)S(1)} %get-tuple-element.57) | data formatting | bytes 1048576 | tf_op jit(solution)/shard_map/broadcast_in_dim | solution.py:125
  190.2 12.3 %reduce.19 = bf16[2048,128]{1,0:T(8,128)(2,1)} reduce(bf16[2048,1,128]{2,1,0:T(2,128)(2,1)S(1)} %bitcast.144, bf16[]{:T(256)} %broadcast.244), dimensions={1}, to_apply=%bitcast.135.reduce_sub_computation | reduce | bytes 1048578
  203.7 21.0 %all_to_all.17 = bf16[64,2,2048]{2,1,0:T(2,128)(2,1)} all-to-all(bf16[64,2,2048]{2,1,0:T(2,128)(2,1)S(1)} %reshape.248), channel_id=1, replica_groups=mesh['dp'=4,'ctx'=64] {'ctx'}, dimensions={0} | all-to-all | bytes 1048576 | tf_op jit(solution)/shard_map/all_to_all | solution.py:129
  228.3 9.6 %bitcast_reduce_fusion = bf16[2048,128]{1,0:T(8,128)(2,1)} fusion(bf16[2048,1,128]{2,1,0:T(2,128)(2,1)S(1)} %reshape.249), kind=kLoop, calls=%fused_computation.201 | loop fusion | bytes 1048576 | tf_op jit(solution)/shard_map/all_to_all | solution.py:129
  247.7 6.2 %multiply_subtract_fusion.1 = (f32[128,32,128]{2,0,1:T(8,128)}, f32[128,32,128]{2,0,1:T(8,128)}, f32[128,32,128]{2,0,1:T(8,128)S(1)}, f32[128,32,128]{2,0,1:T(8,128)}) fusion(f32[128,32,256]{2,0,1:T(8,128)S(1)} %copy-done.4, f32[128,32,256]{2,0,1:T(8,128)} %fusion, f32[128,32,256]{2,0,1:T(8,128)S(1)} %copy-done.6), kind=kLoop, calls=%fused_computation.69 | loop fusion | flops 6815744 | bytes 20971520 | tf_op jit(solution)/shard_map/sub | solution.py:98
  253.9 5.7 %fusion.20 = f32[128,32,256]{2,0,1:T(8,128)S(1)} fusion(f32[128,32,128]{2,0,1:T(8,128)} %get-tuple-element.30, f32[128,32,128]{2,0,1:T(8,128)} %get-tuple-element.29, f32[128,128]{1,0:T(8,128)S(1)} %get-tuple-element.69, f32[128,128]{1,0:T(8,128)S(1)} %get-tuple-element.71, f32[128,128]{1,0:T(8,128)S(1)} %get-tuple-element.70), kind=kOutput, calls=%fused_computation.23 | convolution fusion | flops 3222470656 | bytes 8585216 | tf_op jit(solution)/shard_map/dot_general | solution.py:23
  268.5 5.6 %copy.53 = f32[256,32,128]{0,2,1:T(8,128)} copy(f32[256,32,128]{2,0,1:T(8,128)} %pad_maximum_fusion.1) | data formatting | bytes 8388608 | tf_op jit(solution)/shard_map/concatenate | solution.py:75
  274.1 6.2 %fusion.46 = bf16[64,32,128]{2,0,1:T(8,128)(2,1)S(1)} fusion(f32[256,32,128]{0,2,1:T(8,128)} %copy.53, f32[64,128]{1,0:T(8,128)S(1)} %copy-done.21, f32[64,128]{1,0:T(8,128)S(1)} %copy-done.23), kind=kOutput, calls=%fused_computation.87 | convolution fusion | flops 805601280 | bytes 4784128 | tf_op jit(solution)/shard_map/dot_general | solution.py:23
  281.4 9.5 %all-to-all-start.1 = ((bf16[64,32,128]{2,1,0:T(8,128)(2,1)}), bf16[64,32,128]{2,1,0:T(8,128)(2,1)}, u32[]{:S(2)}, u32[]{:S(2)}) async-start(bf16[64,32,128]{2,1,0:T(8,128)(2,1)} %copy.54), calls=%async_computation.1 | async-start | bytes 1048576 | tf_op jit(solution)/shard_map/all_to_all | solution.py:133
  295.7 6.0 %copy.67 = f32[256,32,128]{0,2,1:T(8,128)} copy(f32[256,32,128]{2,0,1:T(8,128)} %pad_maximum_fusion.3) | data formatting | bytes 8388608 | tf_op jit(solution)/shard_map/concatenate | solution.py:75
  301.7 6.2 %fusion.43 = bf16[64,32,128]{2,0,1:T(8,128)(2,1)S(1)} fusion(f32[256,32,128]{0,2,1:T(8,128)} %copy.67, f32[64,128]{1,0:T(8,128)S(1)} %copy-done.21, f32[64,128]{1,0:T(8,128)S(1)} %copy-done.23), kind=kOutput, calls=%fused_computation.86 | convolution fusion | flops 805863424 | bytes 4784128 | tf_op jit(solution)/shard_map/dot_general | solution.py:23
  309.0 55.1 %all-reduce.2.cloned.1.call-done = bf16[32,8192]{1,0:T(8,128)(2,1)} async-done(((bf16[32,8192]{1,0:T(8,128)(2,1)}), bf16[32,8192]{1,0:T(8,128)(2,1)}) %all-reduce.2.cloned.1.call-update) | async-done | bytes 524304 | tf_op jit(solution)/shard_map/psum | solution.py:163
  368.7 27.9 %multiply_reduce_fusion = (f32[6144]{0:T(1024)}, f32[6144]{0:T(1024)}, f32[6144]{0:T(1024)}, f32[6144]{0:T(1024)}, f32[6144]{0:T(1024)}, /*index=5*/f32[6144]{0:T(1024)}, f32[6144]{0:T(1024)}) fusion(f32[134,6144]{0,1:T(8,128)} %copy-done.2, f32[128,2048]{0,1:T(8,128)S(1)} %get-tuple-element.56, f32[128,2048]{0,1:T(8,128)S(1)} %get-tuple-element.55, ...), kind=kLoop, calls=%fused_computation.50 | loop fusion | flops 12539904 | bytes 25337856 | tf_op jit(solution)/shard_map/reduce_sum | solution.py:159
  428.7 77.5 %psum.15 = f32[7,768]{1,0:T(8,128)} all-reduce(f32[7,768]{1,0:T(8,128)S(1)} %broadcast_multiply_fusion.1), channel_id=1, replica_groups=mesh['dp'=4,'ctx'=64] {'dp','ctx'}, use_global_device_ids=true, to_apply=%region_9.10 | all-reduce | flops 5376 | bytes 43008 | tf_op jit(solution)/shard_map/psum | solution.py:162
  510.8 13.7 %fusion.39 = bf16[1,128,6144]{1,2,0:T(8,128)(2,1)} fusion(f32[134,6144]{0,1:T(8,128)S(1)} %pad_maximum_fusion, f32[6144]{0:T(1024)S(1)} %copy-done.36, f32[6144]{0:T(1024)S(1)} %copy-done.38, f32[6144]{0:T(1024)S(1)} %copy-done.28, f32[6144]{0:T(1024)S(1)} %copy-done.30, f32[6144]{0:T(1024)S(1)} %copy-done.32, f32[6144]{0:T(1024)S(1)} %copy-done.34, ...), kind=kLoop, calls=%fused_computation.82 | loop fusion | flops 12582912 | bytes 23764992 | tf_op jit(solution)/shard_map/broadcast_in_dim | solution.py:155
  (185 shorter events, 146.4 us)
Async XLA Ops:
  7.2 7.7 %copy-start = (f32[32,8192]{1,0:T(8,128)S(1)}, f32[32,8192]{1,0:T(8,128)}, u32[]{:S(2)}) copy-start(f32[32,8192]{1,0:T(8,128)} %param.6) | copy-start | bytes 3145732
  8.2 15.6 %collective-permute-start = (bf16[6,6144]{1,0:T(8,128)(2,1)S(1)}, bf16[6,6144]{1,0:T(8,128)(2,1)S(1)}, u32[]{:S(2)}, u32[]{:S(2)}) collective-permute-start(bf16[6,6144]{1,0:T(8,128)(2,1)S(1)} %slice_bitcast_fusion.2), channel_id=1, source_target_pairs={{0,1},{1,2},{2,3},{3,4},{4,5},{5,6},{6,7},{7,8},{8,9},{9,10},{10,1... | collective-permute-start | bytes 221192 | tf_op jit(solution)/shard_map/ppermute | solution.py:13
  15.1 5.7 %copy-start.39 = (f32[7,768]{1,0:T(8,128)S(1)}, f32[7,768]{1,0:T(8,128)}, u32[]{:S(2)}) copy-start(f32[7,768]{1,0:T(8,128)} %param.5) | copy-start | bytes 64516
  21.2 6.8 %copy-start.25 = (f32[6144]{0:T(1024)}, f32[6144]{0:T(1024)S(1)}, u32[]{:S(2)}) copy-start(f32[6144]{0:T(1024)S(1)} %broadcast_in_dim.48) | copy-start | bytes 73732
  21.6 6.4 %copy-start.27 = (f32[6144]{0:T(1024)}, f32[6144]{0:T(1024)S(1)}, u32[]{:S(2)}) copy-start(f32[6144]{0:T(1024)S(1)} %broadcast_in_dim.56) | copy-start | bytes 73732
  22.0 6.0 %copy-start.29 = (f32[6144]{0:T(1024)}, f32[6144]{0:T(1024)S(1)}, u32[]{:S(2)}) copy-start(f32[6144]{0:T(1024)S(1)} %broadcast_in_dim.54) | copy-start | bytes 73732
  22.4 5.6 %copy-start.31 = (f32[6144]{0:T(1024)}, f32[6144]{0:T(1024)S(1)}, u32[]{:S(2)}) copy-start(f32[6144]{0:T(1024)S(1)} %broadcast_in_dim.52) | copy-start | bytes 73732
  22.7 5.3 copy-start.33
  23.8 16.1 %copy-start.11 = (bf16[1,128,2048]{1,2,0:T(8,128)(2,1)}, bf16[1,128,2048]{1,2,0:T(8,128)(2,1)S(1)}, u32[]{:S(2)}) copy-start(bf16[1,128,2048]{1,2,0:T(8,128)(2,1)S(1)} %copy.55) | copy-start | bytes 1572868
  28.0 11.9 %copy-start.2 = (f32[134,6144]{0,1:T(8,128)}, f32[134,6144]{0,1:T(8,128)S(1)}, u32[]{:S(2)}) copy-start(f32[134,6144]{0,1:T(8,128)S(1)} %maximum_convert_fusion) | copy-start | bytes 9879556
  63.1 31.3 %all-to-all-start.2 = ((bf16[64,2,2048]{2,1,0:T(2,128)(2,1)}), bf16[64,2,2048]{2,1,0:T(2,128)(2,1)}, u32[]{:S(2)}, u32[]{:S(2)}) async-start(bf16[64,2,2048]{2,1,0:T(2,128)(2,1)} %reshape.246), calls=%async_computation.2 | async-start | bytes 1048576 | tf_op jit(solution)/shard_map/all_to_all | solution.py:134
  139.9 5.6 %copy-start.20 = (f32[64,128]{1,0:T(8,128)S(1)}, f32[64,128]{1,0:T(8,128)}, u32[]{:S(2)}) copy-start(f32[64,128]{1,0:T(8,128)} %get-tuple-element.72) | copy-start | bytes 98308
  139.9 5.6 %copy-start.22 = (f32[64,128]{1,0:T(8,128)S(1)}, f32[64,128]{1,0:T(8,128)}, u32[]{:S(2)}) copy-start(f32[64,128]{1,0:T(8,128)} %get-tuple-element.73) | copy-start | bytes 98308
  145.5 36.3 %copy-start.9 = (f32[128,6144]{0,1:T(8,128)S(1)}, f32[128,6144]{0,1:T(8,128)}, u32[]{:S(2)}) copy-start(f32[128,6144]{0,1:T(8,128)} %copy-done.8) | copy-start | bytes 9437188
  242.6 5.0 copy-start.4
  242.6 5.0 copy-start.6
  253.9 5.7 %copy-start.10 = (f32[128,32,128]{2,0,1:T(8,128)S(1)}, f32[128,32,128]{2,0,1:T(8,128)}, u32[]{:S(2)}) copy-start(f32[128,32,128]{2,0,1:T(8,128)} %get-tuple-element.48) | copy-start | bytes 6291460
  268.5 5.6 %copy-start.21 = (f32[64,128]{1,0:T(8,128)S(1)}, f32[64,128]{1,0:T(8,128)}, u32[]{:S(2)}) copy-start(f32[64,128]{1,0:T(8,128)} %get-tuple-element.72) | copy-start | bytes 98308
  268.5 5.6 %copy-start.23 = (f32[64,128]{1,0:T(8,128)S(1)}, f32[64,128]{1,0:T(8,128)}, u32[]{:S(2)}) copy-start(f32[64,128]{1,0:T(8,128)} %get-tuple-element.73) | copy-start | bytes 98308
  281.4 84.8 %all-to-all-start.1 = ((bf16[64,32,128]{2,1,0:T(8,128)(2,1)}), bf16[64,32,128]{2,1,0:T(8,128)(2,1)}, u32[]{:S(2)}, u32[]{:S(2)}) async-start(bf16[64,32,128]{2,1,0:T(8,128)(2,1)} %copy.54), calls=%async_computation.1 | async-start | bytes 1048576 | tf_op jit(solution)/shard_map/all_to_all | solution.py:133
  290.9 73.2 %all-reduce.2.cloned.1.call-start = ((), (), s32[]{:S(2)}) async-start(), calls=%async_computation.4 | async-start | bytes 1048576 | tf_op jit(solution)/shard_map/psum | solution.py:163
  368.7 139.6 %copy-start.7 = (f32[128,2048]{0,1:T(8,128)}, f32[128,2048]{0,1:T(8,128)S(1)}, u32[]{:S(2)}) copy-start(f32[128,2048]{0,1:T(8,128)S(1)} %get-tuple-element.58) | copy-start | bytes 3145732
  413.0 93.2 %collective-permute-start.1 = (bf16[6,6144]{1,0:T(8,128)(2,1)S(1)}, bf16[6,6144]{1,0:T(8,128)(2,1)S(1)}, u32[]{:S(2)}, u32[]{:S(2)}) collective-permute-start(bf16[6,6144]{1,0:T(8,128)(2,1)S(1)} %copy.65), channel_id=1, source_target_pairs={{1,0},{2,1},{3,2},{4,3},{5,4},{6,5},{7,6},{8,7},{9,8},{10,9},{11,1... | collective-permute-start | bytes 221192 | tf_op jit(solution)/shard_map/ppermute | solution.py:13
  510.8 16.3 %copy-start.1 = (f32[32,8192]{1,0:T(8,128)S(1)}, f32[32,8192]{1,0:T(8,128)}, u32[]{:S(2)}) copy-start(f32[32,8192]{1,0:T(8,128)} %param.6) | copy-start | bytes 3145732
  (21 other events, 58.4 us)
Sparse Core Ops, SparseCore 0:
  309.2 54.9 all-reduce.1
where the time goes:
time: 545 us; the launch traced here: 534 us
  local copies, waits for them, and re-layouts  129 us (24%)
  blocking collectives  128 us (23%)
  other arithmetic  120 us (22%)
  waiting for transfers between devices  55.4 us (10%)
  matrix products  53.4 us (10%)
  starting transfers between devices  32.8 us (6%)
  between operations  15.1 us (3%)
    psum x1, blocking collectives, shards(): grad_short = lax.psum(short_terms, ('dp', 'ctx'))  77.5 us
    psum x1, waiting for transfers between devices, shards(): lax.psum(long_terms.astype(jnp.bfloat16), 'dp').astype(jnp.float32)  55.1 us
    dot_general x12, matrix products, matmul(): jnp.dot(left_side, right_side, precision=precise, preferred_element_type=...  53.4 us
    unnamed x97, local copies, waits for them, and re-layouts  30 us
    all_to_all x1, blocking collectives, shards(): lax.all_to_all(du_own, 'ctx', split_axis=0, concat_axis=1, tiled=True)  29.5 us
    reduce_sum x1, other arithmetic, shards(): jnp.sum(grad_short_out * padded[start:start + row_count], axis=0)  27.9 us
    unnamed x2, other arithmetic  24.3 us
    all_to_all x1, blocking collectives, shards(): lax.all_to_all(product, 'ctx', split_axis=1, concat_axis=0, tiled=True)  21 us
  transfers between devices with their start and end apart: 5, of which 2 were waited for; matrix products, arithmetic and copies ran while one was open for 11% of the time, Pallas kernels for 0%

commit v1 on v0

--- a/solution.py
+++ b/solution.py
@@ -159,7 +159,7 @@
         lag_terms.append(jnp.sum(grad_short_out * padded[start : start + row_count], axis=0))
     short_terms = jnp.stack(lag_terms).reshape(tap_count, -1, group_size).sum(axis=2) * grad_scale
     long_terms = dh_own.transpose(1, 0, 2).reshape(own_chans, ctx_count * row_count) * grad_scale
-    grad_short = lax.psum(short_terms, ("dp", "ctx"))
+    grad_short = lax.psum(lax.psum(short_terms, "dp"), "ctx")
     grad_long = lax.psum(long_terms.astype(jnp.bfloat16), "dp").astype(jnp.float32)
     return (mixer_out, grad_qkv, grad_long, grad_short)
 

time: 545 us -> 886 us (1.63)
  the two profiles are of different devices: /device:TPU:1 before, /device:TPU:0 now
where the time goes in v1:
time: 886 us; the launch traced here: 876 us
  blocking collectives  475 us (54%)
  local copies, waits for them, and re-layouts  129 us (15%)
  other arithmetic  120 us (14%)
  waiting for transfers between devices  57.4 us (6%)
  matrix products  53.3 us (6%)
  starting transfers between devices  25.3 us (3%)
  between operations  15.1 us (2%)
    psum x2, blocking collectives, shards(): grad_short = lax.psum(lax.psum(short_terms, 'dp'), 'ctx')  423 us
    psum x1, waiting for transfers between devices, shards(): lax.psum(long_terms.astype(jnp.bfloat16), 'dp').astype(jnp.float32)  57.3 us
    dot_general x12, matrix products, matmul(): jnp.dot(left_side, right_side, precision=precise, preferred_element_type=...  53.3 us
    unnamed x97, local copies, waits for them, and re-layouts  30 us
    all_to_all x1, blocking collectives, shards(): lax.all_to_all(du_own, 'ctx', split_axis=0, concat_axis=1, tiled=True)  29.5 us
    reduce_sum x1, other arithmetic, shards(): jnp.sum(grad_short_out * padded[start:start + row_count], axis=0)  27.9 us
    unnamed x2, other arithmetic  24.3 us
    all_to_all x1, blocking collectives, shards(): lax.all_to_all(product, 'ctx', split_axis=1, concat_axis=0, tiled=True)  22.8 us
  transfers between devices with their start and end apart: 5, of which 1 were waited for; matrix products, arithmetic and copies ran while one was open for 7% of the time, Pallas kernels for 0%

profile of v1, /device:TPU:0, one launch (start us, length us, event | category | flops | bytes accessed | tf_op | source)
XLA Modules:
  0.0 875.6 jit_solution(195296509751398010)
XLA Ops:
  11.9 5.7 fusion.53
  24.8 11.8 %multiply_add_fusion = f32[128,6144]{0,1:T(8,128)S(1)} fusion(f32[134,6144]{0,1:T(8,128)S(1)} %maximum_convert_fusion, f32[6144]{0:T(1024)S(1)} %broadcast_in_dim.60, f32[6144]{0:T(1024)S(1)} %broadcast_in_dim.58, f32[6144]{0:T(1024)S(1)} %broadcast_in_dim.56, f32[6144]{0:T(1024)S(1)} %broadcast_in_dim.54, f32[6144]{0:T(1024)S(1)} %broadcast_in_dim.52, ...), kind=kLoop, calls=%fused_computation.57 | loop fusion | flops 10223616 | bytes 25337856 | tf_op jit(solution)/shard_map/add | solution.py:120
  38.4 8.1 copy.95
  47.0 12.0 %reduce.18 = bf16[2048,128]{1,0:T(8,128)(2,1)S(1)} reduce(bf16[2048,1,128]{2,1,0:T(2,128)(2,1)S(1)} %bitcast.143, bf16[]{:T(256)} %broadcast.244), dimensions={1}, to_apply=%bitcast.134.reduce_sub_computation | reduce | bytes 1048578
  59.9 14.6 %all-to-all-start.2 = ((bf16[64,2,2048]{2,1,0:T(2,128)(2,1)}), bf16[64,2,2048]{2,1,0:T(2,128)(2,1)}, u32[]{:S(2)}, u32[]{:S(2)}) async-start(bf16[64,2,2048]{2,1,0:T(2,128)(2,1)} %reshape.246), calls=%async_computation.2 | async-start | bytes 1048576 | tf_op jit(solution)/shard_map/all_to_all | solution.py:134
  95.0 8.8 %bitcast_reduce_fusion.1 = bf16[2048,128]{1,0:T(8,128)(2,1)S(1)} fusion(bf16[2048,1,128]{2,1,0:T(2,128)(2,1)S(1)} %reshape.247), kind=kLoop, calls=%fused_computation.202 | loop fusion | bytes 1048576 | tf_op jit(solution)/shard_map/all_to_all | solution.py:134
  136.8 5.6 copy.63
  142.5 6.4 fusion.49
  149.2 29.5 %all_to_all.16 = bf16[64,32,128]{2,1,0:T(8,128)(2,1)S(1)} all-to-all(bf16[64,32,128]{2,1,0:T(8,128)(2,1)S(1)} %copy.64), channel_id=1, replica_groups=mesh['dp'=4,'ctx'=64] {'ctx'}, dimensions={0} | all-to-all | bytes 1048576 | tf_op jit(solution)/shard_map/all_to_all | solution.py:139
  178.9 8.1 copy.96
  187.1 12.3 %reduce.19 = bf16[2048,128]{1,0:T(8,128)(2,1)} reduce(bf16[2048,1,128]{2,1,0:T(2,128)(2,1)S(1)} %bitcast.144, bf16[]{:T(256)} %broadcast.244), dimensions={1}, to_apply=%bitcast.135.reduce_sub_computation | reduce | bytes 1048578
  200.6 22.8 %all_to_all.17 = bf16[64,2,2048]{2,1,0:T(2,128)(2,1)} all-to-all(bf16[64,2,2048]{2,1,0:T(2,128)(2,1)S(1)} %reshape.248), channel_id=1, replica_groups=mesh['dp'=4,'ctx'=64] {'ctx'}, dimensions={0} | all-to-all | bytes 1048576 | tf_op jit(solution)/shard_map/all_to_all | solution.py:129
  227.0 9.6 %bitcast_reduce_fusion = bf16[2048,128]{1,0:T(8,128)(2,1)} fusion(bf16[2048,1,128]{2,1,0:T(2,128)(2,1)S(1)} %reshape.249), kind=kLoop, calls=%fused_computation.201 | loop fusion | bytes 1048576 | tf_op jit(solution)/shard_map/all_to_all | solution.py:129
  246.3 6.2 multiply_subtract_fusion.1
  252.5 5.7 fusion.20
  272.7 6.2 fusion.46
  280.0 8.0 all-to-all-start.1
  292.8 6.0 copy.67
  298.8 6.2 fusion.43
  306.2 57.3 %all-reduce.2.cloned.1.call-done = bf16[32,8192]{1,0:T(8,128)(2,1)} async-done(((bf16[32,8192]{1,0:T(8,128)(2,1)}), bf16[32,8192]{1,0:T(8,128)(2,1)}) %all-reduce.2.cloned.1.call-update) | async-done | bytes 524304 | tf_op jit(solution)/shard_map/psum | solution.py:163
  368.1 27.9 %multiply_reduce_fusion = (f32[6144]{0:T(1024)}, f32[6144]{0:T(1024)}, f32[6144]{0:T(1024)}, f32[6144]{0:T(1024)}, f32[6144]{0:T(1024)}, /*index=5*/f32[6144]{0:T(1024)}, f32[6144]{0:T(1024)}) fusion(f32[134,6144]{0,1:T(8,128)} %copy-done.2, f32[128,2048]{0,1:T(8,128)S(1)} %get-tuple-element.56, f32[128,2048]{0,1:T(8,128)S(1)} %get-tuple-element.55, ...), kind=kLoop, calls=%fused_computation.50 | loop fusion | flops 12539904 | bytes 25337856 | tf_op jit(solution)/shard_map/reduce_sum | solution.py:159
  424.8 16.7 %psum.22 = f32[7,768]{1,0:T(8,128)S(1)} all-reduce(f32[7,768]{1,0:T(8,128)S(1)} %broadcast_multiply_fusion.1), channel_id=1, replica_groups=mesh['dp'=4,'ctx'=64] {'dp'}, use_global_device_ids=true, to_apply=%region_9.10 | all-reduce | flops 5376 | bytes 43008 | tf_op jit(solution)/shard_map/psum | solution.py:162
  441.5 406.1 %psum.23 = f32[7,768]{1,0:T(8,128)} all-reduce(f32[7,768]{1,0:T(8,128)S(1)} %psum.22), channel_id=1, replica_groups=mesh['dp'=4,'ctx'=64] {'ctx'}, use_global_device_ids=true, to_apply=%region_10.11 | all-reduce | flops 5376 | bytes 43008 | tf_op jit(solution)/shard_map/psum | solution.py:162
  852.2 13.7 %fusion.39 = bf16[1,128,6144]{1,2,0:T(8,128)(2,1)} fusion(f32[134,6144]{0,1:T(8,128)S(1)} %pad_maximum_fusion, f32[6144]{0:T(1024)S(1)} %copy-done.36, f32[6144]{0:T(1024)S(1)} %copy-done.38, f32[6144]{0:T(1024)S(1)} %copy-done.28, f32[6144]{0:T(1024)S(1)} %copy-done.30, f32[6144]{0:T(1024)S(1)} %copy-done.32, f32[6144]{0:T(1024)S(1)} %copy-done.34, ...), kind=kLoop, calls=%fused_computation.82 | loop fusion | flops 12582912 | bytes 23764992 | tf_op jit(solution)/shard_map/broadcast_in_dim | solution.py:155
  (186 shorter events, 145.0 us)
Async XLA Ops:
  8.2 12.4 %collective-permute-start = (bf16[6,6144]{1,0:T(8,128)(2,1)S(1)}, bf16[6,6144]{1,0:T(8,128)(2,1)S(1)}, u32[]{:S(2)}, u32[]{:S(2)}) collective-permute-start(bf16[6,6144]{1,0:T(8,128)(2,1)S(1)} %slice_bitcast_fusion.2), channel_id=1, source_target_pairs={{0,1},{1,2},{2,3},{3,4},{4,5},{5,6},{6,7},{7,8},{8,9},{9,10},{10,1... | collective-permute-start | bytes 221192 | tf_op jit(solution)/shard_map/ppermute | solution.py:13
  11.8 5.7 copy-start.39
  18.0 6.8 copy-start.25
  18.4 6.4 copy-start.27
  18.7 6.0 copy-start.29
  19.1 5.6 copy-start.31
  19.5 5.3 copy-start.33
  19.9 4.9 copy-start.35
  20.6 16.1 %copy-start.11 = (bf16[1,128,2048]{1,2,0:T(8,128)(2,1)}, bf16[1,128,2048]{1,2,0:T(8,128)(2,1)S(1)}, u32[]{:S(2)}) copy-start(bf16[1,128,2048]{1,2,0:T(8,128)(2,1)S(1)} %copy.55) | copy-start | bytes 1572868
  24.8 11.9 %copy-start.2 = (f32[134,6144]{0,1:T(8,128)}, f32[134,6144]{0,1:T(8,128)S(1)}, u32[]{:S(2)}) copy-start(f32[134,6144]{0,1:T(8,128)S(1)} %maximum_convert_fusion) | copy-start | bytes 9879556
  59.9 31.5 %all-to-all-start.2 = ((bf16[64,2,2048]{2,1,0:T(2,128)(2,1)}), bf16[64,2,2048]{2,1,0:T(2,128)(2,1)}, u32[]{:S(2)}, u32[]{:S(2)}) async-start(bf16[64,2,2048]{2,1,0:T(2,128)(2,1)} %reshape.246), calls=%async_computation.2 | async-start | bytes 1048576 | tf_op jit(solution)/shard_map/all_to_all | solution.py:134
  136.8 5.6 copy-start.20
  136.8 5.6 copy-start.22
  142.5 36.2 %copy-start.9 = (f32[128,6144]{0,1:T(8,128)S(1)}, f32[128,6144]{0,1:T(8,128)}, u32[]{:S(2)}) copy-start(f32[128,6144]{0,1:T(8,128)} %copy-done.8) | copy-start | bytes 9437188
  241.3 4.9 copy-start.4
  241.3 4.9 copy-start.6
  252.5 5.7 copy-start.10
  267.1 5.6 copy-start.21
  267.1 5.6 copy-start.23
  280.0 85.6 %all-to-all-start.1 = ((bf16[64,32,128]{2,1,0:T(8,128)(2,1)}), bf16[64,32,128]{2,1,0:T(8,128)(2,1)}, u32[]{:S(2)}, u32[]{:S(2)}) async-start(bf16[64,32,128]{2,1,0:T(8,128)(2,1)} %copy.54), calls=%async_computation.1 | async-start | bytes 1048576 | tf_op jit(solution)/shard_map/all_to_all | solution.py:133
  288.1 75.5 %all-reduce.2.cloned.1.call-start = ((), (), s32[]{:S(2)}) async-start(), calls=%async_computation.4 | async-start | bytes 1048576 | tf_op jit(solution)/shard_map/psum | solution.py:163
  368.1 481.6 %copy-start.7 = (f32[128,2048]{0,1:T(8,128)}, f32[128,2048]{0,1:T(8,128)S(1)}, u32[]{:S(2)}) copy-start(f32[128,2048]{0,1:T(8,128)S(1)} %get-tuple-element.58) | copy-start | bytes 3145732
  412.4 435.3 %collective-permute-start.1 = (bf16[6,6144]{1,0:T(8,128)(2,1)S(1)}, bf16[6,6144]{1,0:T(8,128)(2,1)S(1)}, u32[]{:S(2)}, u32[]{:S(2)}) collective-permute-start(bf16[6,6144]{1,0:T(8,128)(2,1)S(1)} %copy.65), channel_id=1, source_target_pairs={{1,0},{2,1},{3,2},{4,3},{5,4},{6,5},{7,6},{8,7},{9,8},{10,9},{11,1... | collective-permute-start | bytes 221192 | tf_op jit(solution)/shard_map/ppermute | solution.py:13
  852.2 16.3 %copy-start.1 = (f32[32,8192]{1,0:T(8,128)S(1)}, f32[32,8192]{1,0:T(8,128)}, u32[]{:S(2)}) copy-start(f32[32,8192]{1,0:T(8,128)} %param.6) | copy-start | bytes 3145732
  (21 other events, 58.0 us)
Sparse Core Ops, SparseCore 0:
  306.3 57.1 all-reduce.1
